TPU v7x, 256 devices: a whole 4x4x8 slice. The times are simulated.
256 devices in a mesh: dp: 16 (over y_lo, z), seq: 16 (over x, y_hi, core).
Axes of the slice: x: 4, y: 4 (y_hi: 2, y_lo: 2; y = y_hi * 2 + y_lo), z: 8, core: 2. Of those that a mesh axis runs over, the one named last changes fastest.
Arguments:
- seq_embed: bfloat16 [16, 3072, 1536], P('dp', 'seq'), may hold values from -24 to 24
- w_qkv: bfloat16 [1536, 2304], P('seq'), may hold values from -1 to 1
- upstream: bfloat16 [16, 3072, 768], P('dp', 'seq'), may hold values from -6 to 6
Outputs:
- attended: bfloat16 [16, 3072, 768], P('dp', 'seq')
- grad_input: bfloat16 [16, 3072, 1536], P('dp', 'seq')
- grad_qkv: bfloat16 [1536, 2304], P('seq')
All inputs are finite; a program needn't handle non-finite values.
Results may differ from a plain program's by a relative error of at most 0.04.
Values may be sent and summed in bfloat16 or wider, within the bound.
A program may use at most 128 MiB of HBM per device.

v0:
```python
import math
import jax
import jax.numpy as jnp
from jax import lax
from jax.sharding import PartitionSpec as P

HEADS = 6


def split_heads(block, heads):
    return block.reshape(block.shape[0], heads, block.shape[1] // heads)


def on_device(seq_embed, w_qkv, upstream):
    heads = HEADS
    width = upstream.shape[-1]
    head_dim = width // heads
    score_scale = 1.0 / math.sqrt(head_dim)
    weights = lax.all_gather(w_qkv, "seq", axis=0, tiled=True)
    tokens = seq_embed[0]
    grad_out = upstream[0]
    rows_here = tokens.shape[0]
    projected = jnp.dot(tokens, weights, preferred_element_type=jnp.float32).astype(jnp.bfloat16)
    queries = projected[:, :width]
    keys_here = projected[:, width : 2 * width]
    values_here = projected[:, 2 * width :]
    keys_all, values_all = (
        lax.all_gather(keys_here, "seq", axis=0, tiled=True),
        lax.all_gather(values_here, "seq", axis=0, tiled=True),
    )
    query_heads = split_heads(queries, heads)
    key_heads = split_heads(keys_all, heads)
    value_heads = split_heads(values_all, heads)
    scores = (
        jnp.einsum("qhd,khd->hqk", query_heads, key_heads, preferred_element_type=jnp.float32)
        * score_scale
    )
    peak = jnp.max(scores, axis=-1, keepdims=True)
    log_total = peak[..., 0] + jnp.log(jnp.sum(jnp.exp(scores - peak), axis=-1))
    probs = jnp.exp(scores - log_total[..., None])
    probs_low = probs.astype(jnp.bfloat16)
    attended_heads = jnp.einsum(
        "hqk,khd->qhd", probs_low, value_heads, preferred_element_type=jnp.float32
    ).astype(jnp.bfloat16)
    grad_heads = split_heads(grad_out, heads)
    delta_rows = jnp.sum(
        grad_heads.astype(jnp.float32) * attended_heads.astype(jnp.float32), axis=-1
    )
    grad_probs = jnp.einsum(
        "qhd,khd->hqk", grad_heads, value_heads, preferred_element_type=jnp.float32
    )
    grad_scores = (probs * (grad_probs - delta_rows.T[..., None]) * score_scale).astype(
        jnp.bfloat16
    )
    grad_queries = jnp.einsum(
        "hqk,khd->qhd", grad_scores, key_heads, preferred_element_type=jnp.float32
    ).astype(jnp.bfloat16)
    lse_all, delta_all = (
        lax.all_gather(log_total.T, "seq", axis=0, tiled=True),
        lax.all_gather(delta_rows, "seq", axis=0, tiled=True),
    )
    key_local = split_heads(keys_here, heads)
    value_local = split_heads(values_here, heads)
    query_piece = split_heads(lax.all_gather(queries, "seq", axis=0, tiled=True), heads)
    grad_piece = split_heads(lax.all_gather(grad_out, "seq", axis=0, tiled=True), heads)
    lse_piece = lse_all.T
    delta_piece = delta_all.T
    piece_scores = (
        jnp.einsum("qhd,khd->hqk", query_piece, key_local, preferred_element_type=jnp.float32)
        * score_scale
    )
    piece_probs = jnp.exp(piece_scores - lse_piece[..., None])
    grad_values = jnp.einsum(
        "hqk,qhd->khd",
        piece_probs.astype(jnp.bfloat16),
        grad_piece,
        preferred_element_type=jnp.float32,
    )
    piece_grad_probs = jnp.einsum(
        "qhd,khd->hqk", grad_piece, value_local, preferred_element_type=jnp.float32
    )
    piece_grad_scores = (
        piece_probs * (piece_grad_probs - delta_piece[..., None]) * score_scale
    ).astype(jnp.bfloat16)
    grad_keys = jnp.einsum(
        "hqk,qhd->khd", piece_grad_scores, query_piece, preferred_element_type=jnp.float32
    )
    grad_keys, grad_values = (grad_keys, grad_values)
    grad_proj = jnp.concatenate(
        [
            grad_queries.reshape(rows_here, width),
            grad_keys.astype(jnp.bfloat16).reshape(rows_here, width),
            grad_values.astype(jnp.bfloat16).reshape(rows_here, width),
        ],
        axis=1,
    )
    grad_input = lax.dot_general(
        grad_proj, weights, (((1,), (1,)), ((), ())), preferred_element_type=jnp.float32
    ).astype(jnp.bfloat16)
    term = lax.dot_general(
        tokens, grad_proj, (((0,), (0,)), ((), ())), preferred_element_type=jnp.float32
    )
    summed = lax.psum_scatter(
        lax.optimization_barrier(term.astype(jnp.bfloat16))
        .astype(jnp.float32)
        .astype(jnp.bfloat16),
        "seq",
        scatter_dimension=0,
        tiled=True,
    )
    total = lax.psum(summed, "dp").astype(jnp.float32)
    attended = attended_heads.reshape(rows_here, width)
    return (attended[None], grad_input[None], total.astype(jnp.bfloat16))


def solution(mesh):
    placed = (P("dp", "seq", None), P("seq", None), P("dp", "seq", None))
    return jax.shard_map(
        on_device,
        mesh=mesh,
        in_specs=placed,
        out_specs=(P("dp", "seq", None), P("dp", "seq", None), P("seq", None)),
        check_vma=False,
    )
```

profile of v0, /device:TPU:2, one launch (start us, length us, event | category | flops | bytes accessed | tf_op | source)
XLA Modules:
  0.0 663.6 jit_solution(6117910122317396261)
XLA Ops:
  7.2 0.7 all-gather.9.cloned.1.call-update
  8.0 0.7 all-gather.17.cloned.1.call-update
  8.7 76.5 %all-gather.9.cloned.1.call-done = bf16[1536,2304]{1,0:T(8,128)(2,1)} async-done(((bf16[96,2304]{1,0:T(8,128)(2,1)}), bf16[1536,2304]{1,0:T(8,128)(2,1)}) %all-gather.9.cloned.1.call-update) | async-done | bytes 7077904 | tf_op jit(solution)/shard_map/all_gather | solution.py:19
  85.2 4.5 convolution_convert_fusion.1
  89.7 1.0 slice_bitcast_fusion.2
  90.8 0.5 all-gather.13.cloned.1.call-update
  91.4 0.5 all-gather.15.cloned.1.call-update
  92.3 57.5 %all-gather.17.cloned.1.call-done = bf16[1,3072,768]{2,1,0:T(8,128)(2,1)} async-done(((bf16[1,192,768]{2,1,0:T(8,128)(2,1)}), bf16[1,3072,768]{2,1,0:T(8,128)(2,1)}) %all-gather.17.cloned.1.call-update) | async-done | bytes 4718608 | tf_op jit(solution)/shard_map/all_gather | solution.py:65
  149.8 6.7 %copy.47 = bf16[1,3072,768]{1,2,0:T(8,128)(2,1)} copy(bf16[1,3072,768]{2,1,0:T(8,128)(2,1)} %all-gather.17.cloned.1.call-done) | data formatting | bytes 9437184 | tf_op jit(solution)/shard_map/all_gather | solution.py:65
  156.5 58.5 %all-gather.11.cloned.1.call-done = bf16[3072,768]{1,0:T(8,128)(2,1)} async-done(((bf16[192,768]{1,0:T(8,128)(2,1)}), bf16[3072,768]{1,0:T(8,128)(2,1)}) %all-gather.11.cloned.1.call-update) | async-done | bytes 4718608 | tf_op jit(solution)/shard_map/all_gather | solution.py:29
  215.0 6.7 %copy.32 = bf16[3072,768]{0,1:T(8,128)(2,1)} copy(bf16[3072,768]{1,0:T(8,128)(2,1)} %all-gather.11.cloned.1.call-done) | data formatting | bytes 9437184 | tf_op jit(solution)/shard_map/all_gather | solution.py:29
  221.7 58.3 %all-gather.13.cloned.1.call-done = bf16[3072,768]{1,0:T(8,128)(2,1)} async-done(((bf16[192,768]{1,0:T(8,128)(2,1)}), bf16[3072,768]{1,0:T(8,128)(2,1)}) %all-gather.13.cloned.1.call-update) | async-done | bytes 4718608 | tf_op jit(solution)/shard_map/all_gather | solution.py:28
  280.0 6.7 %copy.33 = bf16[3072,768]{0,1:T(8,128)(2,1)} copy(bf16[3072,768]{1,0:T(8,128)(2,1)} %all-gather.13.cloned.1.call-done) | data formatting | bytes 9437184 | tf_op jit(solution)/shard_map/all_gather | solution.py:28
  286.7 9.6 %multiply_reduce_fusion = (f32[6,192]{1,0:T(8,128)S(1)}, f32[6,192,3072]{2,1,0:T(8,128)}) fusion(bf16[3072,6,128]{0,2,1:T(8,128)(2,1)} %bitcast.94, bf16[24,6,8,128]{3,2,1,0:T(8,128)(2,1)S(1)} %get-tuple-element.13), kind=kOutput, calls=%fused_computation.11 | convolution fusion | flops 913046400 | bytes 19173888 | tf_op jit(solution)/shard_map/qhd,khd->hqk/dot_general | solution.py:35
  296.3 7.5 %exponential_reduce_fusion = f32[6,192]{1,0:T(8,128)S(1)} fusion(f32[6,192,3072]{2,1,0:T(8,128)} %get-tuple-element.19, f32[6,192]{1,0:T(8,128)S(1)} %get-tuple-element.18), kind=kLoop, calls=%fused_computation.8 | loop fusion | flops 10615680 | bytes 14164992 | tf_op jit(solution)/shard_map/reduce_sum | solution.py:39
  303.8 8.5 %multiply_reduce_fusion.1 = (f32[192,6]{0,1:T(8,128)S(1)}, bf16[192,6,128]{2,0,1:T(8,128)(2,1)}) fusion(bf16[192,6,128]{2,1,0:T(8,128)(2,1)S(1)} %reshape_squeeze.3, bf16[3072,6,128]{0,2,1:T(8,128)(2,1)S(1)} %bitcast.103, f32[6,192,3072]{2,1,0:T(8,128)} %get-tuple-element.19, f32[6,192]{1,0:T(8,128)S(1)} %log_add_fusion), kind=kOutput, calls=%fused_computation.37 | convolution fusion | flops 917322624 | bytes 19473408 | tf_op jit(solution)/shard_map/hqk,khd->qhd/dot_general | solution.py:42
  312.3 20.3 %all-gather.2 = f32[16,192,6]{1,2,0:T(8,128)S(1)} all-gather(f32[1,192,6]{1,2,0:T(8,128)S(1)} %bitcast.108), channel_id=1, replica_groups=mesh['dp'=16,'seq'=16] {'seq'}, dimensions={0}, use_global_device_ids=true | all-gather | bytes 78336 | tf_op jit(solution)/shard_map/all_gather | solution.py:60
  332.8 20.5 %all-gather.1 = f32[16,192,6]{1,2,0:T(8,128)S(1)} all-gather(f32[1,192,6]{1,2,0:T(8,128)S(1)} %bitcast.107), channel_id=1, replica_groups=mesh['dp'=16,'seq'=16] {'seq'}, dimensions={0}, use_global_device_ids=true | all-gather | bytes 78336 | tf_op jit(solution)/shard_map/all_gather | solution.py:59
  353.5 10.7 %fusion.42 = bf16[6,24,8,128]{3,2,1,0:T(8,128)(2,1)S(1)} fusion(bf16[3072,6,128]{0,2,1:T(8,128)(2,1)} %bitcast.95, f32[6,192,3072]{2,1,0:T(8,128)} %get-tuple-element.19, f32[6,192]{1,0:T(8,128)S(1)} %bitcast.109, f32[6,192]{1,0:T(8,128)S(1)} %log_add_fusion, bf16[3072,6,128]{0,2,1:T(8,128)(2,1)} %bitcast.100, bf16[192,6,128]{2,1,0:T(8,128)(2,1)S(1)} %reshape_squeeze.3), kind=kOutput, calls=%fused_computation.33 | convolution fusion | flops 1833320448 | bytes 24192000 | tf_op jit(solution)/shard_map/hqk,khd->qhd/dot_general | solution.py:55
  364.3 6.7 %copy.43 = bf16[3072,768]{0,1:T(8,128)(2,1)} copy(bf16[3072,768]{1,0:T(8,128)(2,1)} %all-gather.15.cloned.1.call-done) | data formatting | bytes 9437184 | tf_op jit(solution)/shard_map/all_gather | solution.py:64
  371.0 9.4 %fusion.54 = f32[6,3072,192]{1,2,0:T(8,128)} fusion(bf16[3072,6,128]{0,2,1:T(8,128)(2,1)} %bitcast.96, bf16[24,6,8,128]{3,2,1,0:T(8,128)(2,1)S(1)} %get-tuple-element.14), kind=kOutput, calls=%fused_computation.43 | convolution fusion | flops 905969664 | bytes 19169280 | tf_op jit(solution)/shard_map/qhd,khd->hqk/dot_general | solution.py:69
  380.3 8.8 %fusion.36 = bf16[6,24,8,128]{3,2,1,0:T(8,128)(2,1)S(1)} fusion(bf16[3072,6,128]{0,2,1:T(8,128)(2,1)} %bitcast.98, f32[6,3072,192]{1,2,0:T(8,128)} %fusion.54, f32[6,3072]{1,0:T(8,128)S(1)} %bitcast.105), kind=kOutput, calls=%fused_computation.31 | convolution fusion | flops 916733952 | bytes 19243008 | tf_op jit(solution)/shard_map/hqk,qhd->khd/dot_general | solution.py:73
  389.1 10.9 %fusion.45 = bf16[6,24,8,128]{3,2,1,0:T(8,128)(2,1)S(1)} fusion(bf16[3072,6,128]{0,2,1:T(8,128)(2,1)} %bitcast.97, f32[6,3072,192]{1,2,0:T(8,128)} %fusion.54, f32[6,3072]{1,0:T(8,128)S(1)} %bitcast.104, f32[6,3072]{1,0:T(8,128)} %bitcast.106, bf16[3072,6,128]{0,2,1:T(8,128)(2,1)} %bitcast.99, bf16[24,6,8,128]{3,2,1,0:T(8,128)(2,1)S(1)} %get-tuple-element.12), kind=kOutput, calls=%fused_computation.34 | convolution fusion | flops 1833320448 | bytes 24330240 | tf_op jit(solution)/shard_map/hqk,qhd->khd/dot_general | solution.py:85
  400.1 5.0 fusion.6
  405.1 9.8 %copy.64 = bf16[1536,2304]{1,0:T(8,128)(2,1)} copy(bf16[1536,2304]{0,1:T(8,128)(2,1)} %fusion.6) | data formatting | bytes 14155776
  415.0 0.9 copy-done.2
  416.1 1.1 broadcast_in_dim_reshape.3
  417.1 99.5 %reduce-scatter.4.cloned.1.call-done = bf16[96,2304]{1,0:T(8,128)(2,1)} async-done(((bf16[1536,2304]{1,0:T(8,128)(2,1)}), bf16[96,2304]{1,0:T(8,128)(2,1)}) %reduce-scatter.4.cloned.1.call-update) | async-done | bytes 442384
  516.7 2.1 copy.65
  518.8 6.3 fusion.23
  525.0 129.7 %all-reduce.2.cloned.1.call-done = bf16[96,2304]{0,1:T(8,128)(2,1)} async-done(((bf16[96,2304]{0,1:T(8,128)(2,1)}), bf16[96,2304]{0,1:T(8,128)(2,1)}) %all-reduce.2.cloned.1.call-update) | async-done | bytes 442384 | tf_op jit(solution)/shard_map/psum | solution.py:111
  654.7 2.1 copy.55
  (33 shorter events, 1.3 us)
Async XLA Ops:
  7.2 78.0 %copy-start = (bf16[1,192,1536]{2,1,0:T(8,128)(2,1)S(1)}, bf16[1,192,1536]{2,1,0:T(8,128)(2,1)}, u32[]{:S(2)}) copy-start(bf16[1,192,1536]{2,1,0:T(8,128)(2,1)} %param.3) | copy-start | bytes 1769476
  7.2 78.0 %all-gather.9.cloned.1.call-start = ((), (), s32[]{:S(2)}) async-start(), calls=%async_computation.1 | async-start | bytes 7520256 | tf_op jit(solution)/shard_map/all_gather | solution.py:19
  7.9 141.9 %all-gather.17.cloned.1.call-start = ((), (), s32[]{:S(2)}) async-start(), calls=%async_computation.6 | async-start | bytes 5013504 | tf_op jit(solution)/shard_map/all_gather | solution.py:65
  8.7 83.3 %copy-start.1 = (bf16[1,192,768]{2,1,0:T(8,128)(2,1)S(1)}, bf16[1,192,768]{2,1,0:T(8,128)(2,1)}, u32[]{:S(2)}) copy-start(bf16[1,192,768]{2,1,0:T(8,128)(2,1)} %param.5) | copy-start | bytes 884740
  8.7 206.3 %all-gather.11.cloned.1.call-start = ((), (), s32[]{:S(2)}) async-start(), calls=%async_computation.2 | async-start | bytes 5013504 | tf_op jit(solution)/shard_map/all_gather | solution.py:29
  90.8 189.2 %all-gather.13.cloned.1.call-start = ((), (), s32[]{:S(2)}) async-start(), calls=%async_computation.3 | async-start | bytes 5013504 | tf_op jit(solution)/shard_map/all_gather | solution.py:28
  91.3 272.9 %all-gather.15.cloned.1.call-start = ((), (), s32[]{:S(2)}) async-start(), calls=%async_computation.4 | async-start | bytes 5013504 | tf_op jit(solution)/shard_map/all_gather | solution.py:64
  91.9 424.7 %reduce-scatter.4.cloned.1.call-start = ((), (), s32[]{:S(2)}) async-start(), calls=%async_computation.7 | async-start | bytes 7520256
  280.0 23.8 %slice-start = ((s8[4718592]{0:T(1024)(128)(4,1)}), s8[524288]{0:T(1024)(128)(4,1)S(1)}, s32[]{:S(2)}) async-start(s8[4718592]{0:T(1024)(128)(4,1)} %bitcast.101), calls=%async_computation.8 | async-start | bytes 1048576
  286.7 17.1 %slice-start.1 = ((s8[4718592]{0:T(1024)(128)(4,1)}), s8[4194304]{0:T(1024)(128)(4,1)S(1)}, s32[]{:S(2)}) async-start(s8[4718592]{0:T(1024)(128)(4,1)} %bitcast.101), calls=%async_computation.9 | async-start | bytes 8388608
  353.5 26.9 %copy-start.3 = (f32[3072,6]{0,1:T(8,128)}, f32[3072,6]{0,1:T(8,128)S(1)}, u32[]{:S(2)}) copy-start(f32[3072,6]{0,1:T(8,128)S(1)} %reshape.59) | copy-start | bytes 221188
  414.9 1.0 copy-start.2
  414.9 239.8 %all-reduce.2.cloned.1.call-start = ((), (), s32[]{:S(2)}) async-start(), calls=%async_computation.5 | async-start | bytes 1179648 | tf_op jit(solution)/shard_map/psum | solution.py:111
Sparse Core Ops, SparseCore 0:
  10.7 74.4 all-gather.8
  87.9 61.8 all-gather.16
  153.1 61.8 all-gather.10
  218.1 61.8 all-gather.12
  283.1 62.3 all-gather.14
  415.0 101.5 reduce-scatter.3
  519.3 135.3 all-reduce.1
where the time goes:
time: 665 us; the launch traced here: 664 us
  waiting for transfers between devices  482 us (72%)
  matrix products  73.6 us (11%)
  local copies, waits for them, and re-layouts  44.6 us (7%)
  blocking collectives  40.9 us (6%)
  between operations  14.3 us (2%)
  other arithmetic  7.47 us (1%)
    psum x1, waiting for transfers between devices, on_device(): total = lax.psum(summed, 'dp').astype(jnp.float32)  130 us
    unnamed x8, waiting for transfers between devices  102 us
    all_gather x1, waiting for transfers between devices, on_device(): weights = lax.all_gather(w_qkv, 'seq', axis=0, tiled=True)  76.5 us
    all_gather x1, waiting for transfers between devices, on_device(): lax.all_gather(values_here, 'seq', axis=0, tiled=True)  58.5 us
    all_gather x1, waiting for transfers between devices, on_device(): lax.all_gather(keys_here, 'seq', axis=0, tiled=True)  58.3 us
    all_gather x1, waiting for transfers between devices, on_device(): lax.all_gather(grad_out, 'seq', axis=0, tiled=True)  57.5 us
    all_gather x1, blocking collectives, on_device(): lax.all_gather(log_total.T, 'seq', axis=0, tiled=True)  20.5 us
    all_gather x1, blocking collectives, on_device(): lax.all_gather(delta_rows, 'seq', axis=0, tiled=True)  20.3 us
  transfers between devices with their start and end apart: 7, of which 6 were waited for; matrix products, arithmetic and copies ran while one was open for 11% of the time, Pallas kernels for 0%

commit v1 on v0

--- a/solution.py
+++ b/solution.py
@@ -16,7 +16,9 @@
     width = upstream.shape[-1]
     head_dim = width // heads
     score_scale = 1.0 / math.sqrt(head_dim)
-    weights = lax.all_gather(w_qkv, "seq", axis=0, tiled=True)
+    weights = jnp.concatenate(
+        lax.all_to_all(jnp.stack([w_qkv] * lax.axis_size("seq")), "seq", 0, 0), axis=0
+    )
     tokens = seq_embed[0]
     grad_out = upstream[0]
     rows_here = tokens.shape[0]

time: 665 us -> 638 us (0.959)
  waiting for transfers between devices: 482 us -> 359 us
  blocking collectives: 40.9 us -> 138 us
    all_to_all x0 -> x1, blocking collectives: none -> 96.8 us  [on_device(): lax.all_to_all(jnp.stack([w_qkv] * lax.axis_size('seq')), 'seq', 0, 0)]
    all_gather x1 -> x0, waiting for transfers between devices: 76.5 us -> none  [on_device(): weights = lax.all_gather(w_qkv, 'seq', axis=0, tiled=True)]
    all_gather x1, waiting for transfers between devices: 57.5 us -> 10.3 us  [on_device(): lax.all_gather(grad_out, 'seq', axis=0, tiled=True)]
    unnamed x20 -> x22, local copies, waits for them, and re-layouts: 16.1 us -> 17.5 us
    unnamed x8 -> x7, waiting for transfers between devices: 102 us -> 101 us
  transfers between devices with their start and end apart: 7 -> 6, of which waited for: 6 -> 5; matrix products, arithmetic and copies ran while one was open for 11% -> 11% of each run, Pallas kernels for 0% -> 0%
where the time goes in v1:
time: 638 us; the launch traced here: 637 us
  waiting for transfers between devices  359 us (56%)
  blocking collectives  138 us (22%)
  matrix products  70.6 us (11%)
  local copies, waits for them, and re-layouts  47.7 us (7%)
  between operations  14.3 us (2%)
  other arithmetic  7.47 us (1%)
    psum x1, waiting for transfers between devices, on_device(): total = lax.psum(summed, 'dp').astype(jnp.float32)  130 us
    unnamed x7, waiting for transfers between devices  101 us
    all_to_all x1, blocking collectives, on_device(): lax.all_to_all(jnp.stack([w_qkv] * lax.axis_size('seq')), 'seq', 0, 0)  96.8 us
    all_gather x1, waiting for transfers between devices, on_device(): lax.all_gather(values_here, 'seq', axis=0, tiled=True)  59.4 us
    all_gather x1, waiting for transfers between devices, on_device(): lax.all_gather(keys_here, 'seq', axis=0, tiled=True)  58.5 us
    all_gather x1, blocking collectives, on_device(): lax.all_gather(log_total.T, 'seq', axis=0, tiled=True)  20.5 us
    all_gather x1, blocking collectives, on_device(): lax.all_gather(delta_rows, 'seq', axis=0, tiled=True)  20.4 us
    unnamed x22, local copies, waits for them, and re-layouts  17.5 us
  transfers between devices with their start and end apart: 6, of which 5 were waited for; matrix products, arithmetic and copies ran while one was open for 11% of the time, Pallas kernels for 0%

profile of v1, /device:TPU:2, one launch (start us, length us, event | category | flops | bytes accessed | tf_op | source)
XLA Modules:
  0.0 637.1 jit_solution(16806106186365798912)
XLA Ops:
  7.2 0.7 all-gather.14.cloned.1.call-update
  8.0 1.7 stack.2
  9.7 96.8 %all_to_all.5 = bf16[16,96,2304]{2,1,0:T(8,128)(2,1)S(1)} all-to-all(bf16[16,96,2304]{2,1,0:T(8,128)(2,1)S(1)} %stack.2), channel_id=1, replica_groups=mesh['dp'=16,'seq'=16] {'seq'}, dimensions={0} | all-to-all | bytes 14155776 | tf_op jit(solution)/shard_map/all_to_all | solution.py:20
  106.5 1.5 convolution_convert_fusion.1
  108.1 1.3 copy-done.1
  109.3 1.0 slice_bitcast_fusion.2
  110.4 0.7 all-gather.10.cloned.1.call-update
  112.1 10.3 %all-gather.14.cloned.1.call-done = bf16[1,3072,768]{2,1,0:T(8,128)(2,1)} async-done(((bf16[1,192,768]{2,1,0:T(8,128)(2,1)}), bf16[1,3072,768]{2,1,0:T(8,128)(2,1)}) %all-gather.14.cloned.1.call-update) | async-done | bytes 4718608 | tf_op jit(solution)/shard_map/all_gather | solution.py:67
  122.3 6.7 %copy.47 = bf16[1,3072,768]{1,2,0:T(8,128)(2,1)} copy(bf16[1,3072,768]{2,1,0:T(8,128)(2,1)} %all-gather.14.cloned.1.call-done) | data formatting | bytes 9437184 | tf_op jit(solution)/shard_map/all_gather | solution.py:67
  129.0 59.4 %all-gather.8.cloned.1.call-done = bf16[3072,768]{1,0:T(8,128)(2,1)} async-done(((bf16[192,768]{1,0:T(8,128)(2,1)}), bf16[3072,768]{1,0:T(8,128)(2,1)}) %all-gather.8.cloned.1.call-update) | async-done | bytes 4718608 | tf_op jit(solution)/shard_map/all_gather | solution.py:31
  188.5 6.7 %copy.32 = bf16[3072,768]{0,1:T(8,128)(2,1)} copy(bf16[3072,768]{1,0:T(8,128)(2,1)} %all-gather.8.cloned.1.call-done) | data formatting | bytes 9437184 | tf_op jit(solution)/shard_map/all_gather | solution.py:31
  195.2 58.5 %all-gather.10.cloned.1.call-done = bf16[3072,768]{1,0:T(8,128)(2,1)} async-done(((bf16[192,768]{1,0:T(8,128)(2,1)}), bf16[3072,768]{1,0:T(8,128)(2,1)}) %all-gather.10.cloned.1.call-update) | async-done | bytes 4718608 | tf_op jit(solution)/shard_map/all_gather | solution.py:30
  253.7 6.7 %copy.33 = bf16[3072,768]{0,1:T(8,128)(2,1)} copy(bf16[3072,768]{1,0:T(8,128)(2,1)} %all-gather.10.cloned.1.call-done) | data formatting | bytes 9437184 | tf_op jit(solution)/shard_map/all_gather | solution.py:30
  260.4 9.6 %multiply_reduce_fusion = (f32[6,192]{1,0:T(8,128)S(1)}, f32[6,192,3072]{2,1,0:T(8,128)}) fusion(bf16[3072,6,128]{0,2,1:T(8,128)(2,1)} %bitcast.95, bf16[24,6,8,128]{3,2,1,0:T(8,128)(2,1)S(1)} %get-tuple-element.13), kind=kOutput, calls=%fused_computation.11 | convolution fusion | flops 913046400 | bytes 19173888 | tf_op jit(solution)/shard_map/qhd,khd->hqk/dot_general | solution.py:37
  270.0 7.5 %exponential_reduce_fusion = f32[6,192]{1,0:T(8,128)S(1)} fusion(f32[6,192,3072]{2,1,0:T(8,128)} %get-tuple-element.19, f32[6,192]{1,0:T(8,128)S(1)} %get-tuple-element.18), kind=kLoop, calls=%fused_computation.8 | loop fusion | flops 10615680 | bytes 14164992 | tf_op jit(solution)/shard_map/reduce_sum | solution.py:41
  277.5 8.5 %multiply_reduce_fusion.1 = (f32[192,6]{0,1:T(8,128)S(1)}, bf16[192,6,128]{2,0,1:T(8,128)(2,1)}) fusion(bf16[192,6,128]{2,1,0:T(8,128)(2,1)S(1)} %reshape_squeeze.3, bf16[3072,6,128]{0,2,1:T(8,128)(2,1)S(1)} %bitcast.106, f32[6,192,3072]{2,1,0:T(8,128)} %get-tuple-element.19, f32[6,192]{1,0:T(8,128)S(1)} %log_add_fusion), kind=kOutput, calls=%fused_computation.37 | convolution fusion | flops 917322624 | bytes 19473408 | tf_op jit(solution)/shard_map/hqk,khd->qhd/dot_general | solution.py:44
  286.0 20.4 %all-gather.2 = f32[16,192,6]{1,2,0:T(8,128)S(1)} all-gather(f32[1,192,6]{1,2,0:T(8,128)S(1)} %bitcast.111), channel_id=1, replica_groups=mesh['dp'=16,'seq'=16] {'seq'}, dimensions={0}, use_global_device_ids=true | all-gather | bytes 78336 | tf_op jit(solution)/shard_map/all_gather | solution.py:62
  306.5 20.5 %all-gather.1 = f32[16,192,6]{1,2,0:T(8,128)S(1)} all-gather(f32[1,192,6]{1,2,0:T(8,128)S(1)} %bitcast.110), channel_id=1, replica_groups=mesh['dp'=16,'seq'=16] {'seq'}, dimensions={0}, use_global_device_ids=true | all-gather | bytes 78336 | tf_op jit(solution)/shard_map/all_gather | solution.py:61
  327.1 10.7 %fusion.42 = bf16[6,24,8,128]{3,2,1,0:T(8,128)(2,1)S(1)} fusion(bf16[3072,6,128]{0,2,1:T(8,128)(2,1)} %bitcast.96, f32[6,192,3072]{2,1,0:T(8,128)} %get-tuple-element.19, f32[6,192]{1,0:T(8,128)S(1)} %bitcast.112, f32[6,192]{1,0:T(8,128)S(1)} %log_add_fusion, bf16[3072,6,128]{0,2,1:T(8,128)(2,1)} %bitcast.103, bf16[192,6,128]{2,1,0:T(8,128)(2,1)S(1)} %reshape_squeeze.3), kind=kOutput, calls=%fused_computation.33 | convolution fusion | flops 1833320448 | bytes 24192000 | tf_op jit(solution)/shard_map/hqk,khd->qhd/dot_general | solution.py:57
  337.9 6.7 %copy.43 = bf16[3072,768]{0,1:T(8,128)(2,1)} copy(bf16[3072,768]{1,0:T(8,128)(2,1)} %all-gather.12.cloned.1.call-done) | data formatting | bytes 9437184 | tf_op jit(solution)/shard_map/all_gather | solution.py:66
  344.6 9.4 %fusion.54 = f32[6,3072,192]{1,2,0:T(8,128)} fusion(bf16[3072,6,128]{0,2,1:T(8,128)(2,1)} %bitcast.97, bf16[24,6,8,128]{3,2,1,0:T(8,128)(2,1)S(1)} %get-tuple-element.14), kind=kOutput, calls=%fused_computation.43 | convolution fusion | flops 905969664 | bytes 19169280 | tf_op jit(solution)/shard_map/qhd,khd->hqk/dot_general | solution.py:71
  354.0 8.8 %fusion.36 = bf16[6,24,8,128]{3,2,1,0:T(8,128)(2,1)S(1)} fusion(bf16[3072,6,128]{0,2,1:T(8,128)(2,1)} %bitcast.101, f32[6,3072,192]{1,2,0:T(8,128)} %fusion.54, f32[6,3072]{1,0:T(8,128)S(1)} %bitcast.108), kind=kOutput, calls=%fused_computation.31 | convolution fusion | flops 916733952 | bytes 19243008 | tf_op jit(solution)/shard_map/hqk,qhd->khd/dot_general | solution.py:75
  362.7 10.9 %fusion.45 = bf16[6,24,8,128]{3,2,1,0:T(8,128)(2,1)S(1)} fusion(bf16[3072,6,128]{0,2,1:T(8,128)(2,1)} %bitcast.98, f32[6,3072,192]{1,2,0:T(8,128)} %fusion.54, f32[6,3072]{1,0:T(8,128)S(1)} %bitcast.107, f32[6,3072]{1,0:T(8,128)} %bitcast.109, bf16[3072,6,128]{0,2,1:T(8,128)(2,1)} %bitcast.102, bf16[24,6,8,128]{3,2,1,0:T(8,128)(2,1)S(1)} %get-tuple-element.12), kind=kOutput, calls=%fused_computation.34 | convolution fusion | flops 1833320448 | bytes 24330240 | tf_op jit(solution)/shard_map/hqk,qhd->khd/dot_general | solution.py:87
  373.7 5.0 fusion.6
  378.7 9.9 %copy.64 = bf16[1536,2304]{1,0:T(8,128)(2,1)} copy(bf16[1536,2304]{0,1:T(8,128)(2,1)} %fusion.6) | data formatting | bytes 14155776
  388.7 0.9 copy-done.3
  389.8 1.1 broadcast_in_dim_reshape.3
  390.9 99.4 %reduce-scatter.4.cloned.1.call-done = bf16[96,2304]{1,0:T(8,128)(2,1)} async-done(((bf16[1536,2304]{1,0:T(8,128)(2,1)}), bf16[96,2304]{1,0:T(8,128)(2,1)}) %reduce-scatter.4.cloned.1.call-update) | async-done | bytes 442384
  490.3 2.1 copy.65
  492.4 6.3 fusion.23
  498.6 129.5 %all-reduce.2.cloned.1.call-done = bf16[96,2304]{0,1:T(8,128)(2,1)} async-done(((bf16[96,2304]{0,1:T(8,128)(2,1)}), bf16[96,2304]{0,1:T(8,128)(2,1)}) %all-reduce.2.cloned.1.call-update) | async-done | bytes 442384 | tf_op jit(solution)/shard_map/psum | solution.py:113
  628.1 2.1 copy.55
  (34 shorter events, 1.8 us)
Async XLA Ops:
  7.2 99.3 %copy-start = (bf16[1,192,1536]{2,1,0:T(8,128)(2,1)S(1)}, bf16[1,192,1536]{2,1,0:T(8,128)(2,1)}, u32[]{:S(2)}) copy-start(bf16[1,192,1536]{2,1,0:T(8,128)(2,1)} %param.3) | copy-start | bytes 1769476
  7.2 115.2 %all-gather.14.cloned.1.call-start = ((), (), s32[]{:S(2)}) async-start(), calls=%async_computation.6 | async-start | bytes 5013504 | tf_op jit(solution)/shard_map/all_gather | solution.py:67
  7.9 180.6 %all-gather.8.cloned.1.call-start = ((), (), s32[]{:S(2)}) async-start(), calls=%async_computation.2 | async-start | bytes 5013504 | tf_op jit(solution)/shard_map/all_gather | solution.py:31
  106.5 2.8 copy-start.1
  106.5 5.2 copy-start.2
  110.3 143.3 %all-gather.10.cloned.1.call-start = ((), (), s32[]{:S(2)}) async-start(), calls=%async_computation.3 | async-start | bytes 5013504 | tf_op jit(solution)/shard_map/all_gather | solution.py:30
  111.1 226.8 %all-gather.12.cloned.1.call-start = ((), (), s32[]{:S(2)}) async-start(), calls=%async_computation.4 | async-start | bytes 5013504 | tf_op jit(solution)/shard_map/all_gather | solution.py:66
  111.7 378.6 %reduce-scatter.4.cloned.1.call-start = ((), (), s32[]{:S(2)}) async-start(), calls=%async_computation.7 | async-start | bytes 7520256
  253.7 23.8 %slice-start = ((s8[4718592]{0:T(1024)(128)(4,1)}), s8[524288]{0:T(1024)(128)(4,1)S(1)}, s32[]{:S(2)}) async-start(s8[4718592]{0:T(1024)(128)(4,1)} %bitcast.104), calls=%async_computation.8 | async-start | bytes 1048576
  260.4 17.1 %slice-start.1 = ((s8[4718592]{0:T(1024)(128)(4,1)}), s8[4194304]{0:T(1024)(128)(4,1)S(1)}, s32[]{:S(2)}) async-start(s8[4718592]{0:T(1024)(128)(4,1)} %bitcast.104), calls=%async_computation.9 | async-start | bytes 8388608
  327.1 26.9 %copy-start.4 = (f32[3072,6]{0,1:T(8,128)}, f32[3072,6]{0,1:T(8,128)S(1)}, u32[]{:S(2)}) copy-start(f32[3072,6]{0,1:T(8,128)S(1)} %reshape.65) | copy-start | bytes 221188
  388.6 1.0 copy-start.3
  388.6 239.5 %all-reduce.2.cloned.1.call-start = ((), (), s32[]{:S(2)}) async-start(), calls=%async_computation.5 | async-start | bytes 1179648 | tf_op jit(solution)/shard_map/psum | solution.py:113
Sparse Core Ops, SparseCore 0:
  10.7 111.5 all-gather.13
  125.6 62.8 all-gather.7
  191.8 61.8 all-gather.9
  256.8 62.3 all-gather.11
  388.8 101.4 reduce-scatter.3
  492.8 135.3 all-reduce.1
